TPU v7x, 32 devices: a whole 2x2x4 slice. The times are simulated.
32 devices in a mesh: groups: 2 (over y), tensor: 4 (over z), dp: 2 (over x), pair: 2 (over core).
Axes of the slice: x: 2, y: 2, z: 4, core: 2. Of those that a mesh axis runs over, the one named last changes fastest.
Arguments:
- tokens: bfloat16 [1024, 8192], P(('groups', 'dp', 'tensor')), parts along dimension 0, may hold values from -200 to 200
- time_order: int32 [1024], P(('groups', 'dp')), parts along dimension 0, may hold values from 0 to 255, as said below
- modality: int32 [1024], P(('groups', 'dp')), parts along dimension 0, may hold values 0 or 1
- norm_gain: float32 [2, 8192], replicated, may hold values from 0.5 to 2
- gate_weight: bfloat16 [8192, 16384], P('dp', ('tensor', 'pair')), may hold values from -0.0625 to 0.0625
- up_weight: bfloat16 [8192, 16384], P('dp', ('tensor', 'pair')), may hold values from -0.0625 to 0.0625
- down_weight: bfloat16 [16384, 8192], P(('tensor', 'pair'), 'dp'), may hold values from -0.046875 to 0.046875
Outputs:
- branch_out: bfloat16 [1024, 8192], P(('groups', 'dp', 'tensor', 'pair')), parts along dimension 0
There are 2 independent parts, one for each index of `groups`. A program takes and returns all parts, laid end to end along the dimension named above; an argument that names none is the same for every part. Nothing has to cross between parts.
Inputs may be any that keep to these rules, and one draw needn't show every extreme that they name: `time_order`: within each aligned block of 256 rows, a permutation of 0 to 255.
All inputs are finite; a program needn't handle non-finite values. No bound on the sum of `modality` on one device may be relied on, other than what follows from the above.
Results may differ from a plain program's by a relative error of at most 0.014.
Values may be sent and summed in bfloat16 or wider, within the bound.
A program may use at most 320 MiB of HBM per device.

v0:
```python
import jax
import jax.numpy as jnp
from jax import lax
from jax.sharding import PartitionSpec as P

EPSILON = 1e-05


def normalize(block_rows, row_kinds, norm_gain):
    values = block_rows.astype(jnp.float32)
    inverse_rms = lax.rsqrt(jnp.mean(values * values, axis=1, keepdims=True) + EPSILON)
    chosen = jnp.where(row_kinds[:, None] == 1, norm_gain[1][None, :], norm_gain[0][None, :])
    return (values * inverse_rms * chosen).astype(jnp.bfloat16)


def per_device(tokens, time_order, modality, norm_gain, gate_weight, up_weight, down_weight):
    whole_rows = lax.all_gather(tokens, "tensor", axis=0, tiled=True)
    sorted_rows = jnp.take(whole_rows, time_order, axis=0)
    row_kinds = jnp.take(modality, time_order, axis=0)
    normed = normalize(sorted_rows, row_kinds, norm_gain)
    gate_proj = jnp.dot(
        normed,
        lax.all_gather(gate_weight, "dp", axis=0, tiled=True),
        preferred_element_type=jnp.float32,
    )
    up_proj = jnp.dot(
        normed,
        lax.all_gather(up_weight, "dp", axis=0, tiled=True),
        preferred_element_type=jnp.float32,
    )
    hidden = (jax.nn.silu(gate_proj) * up_proj).astype(jnp.bfloat16)
    down_whole = lax.all_gather(down_weight, "dp", axis=1, tiled=True)
    return lax.psum_scatter(
        jnp.dot(hidden, down_whole, preferred_element_type=jnp.float32).astype(jnp.bfloat16),
        ("tensor", "pair"),
        scatter_dimension=0,
        tiled=True,
    )


def solution(mesh):
    placed = (
        P(("groups", "dp", "tensor"), None),
        P(("groups", "dp")),
        P(("groups", "dp")),
        P(),
        P("dp", ("tensor", "pair")),
        P("dp", ("tensor", "pair")),
        P(("tensor", "pair"), "dp"),
    )
    return jax.shard_map(
        per_device,
        mesh=mesh,
        in_specs=placed,
        out_specs=P(("groups", "dp", "tensor", "pair"), None),
        check_vma=False,
    )
```

profile of v0, /device:TPU:0, one launch (start us, length us, event | category | flops | bytes accessed | tf_op | source)
XLA Modules:
  0.0 1334.4 jit_solution(15386854653368340939)
XLA Ops:
  6.5 0.0 copy-start
  6.5 0.0 all-gather.5.cloned.1.call-start
  6.5 0.7 all-gather.5.cloned.1.call-update
  7.3 0.0 all-gather.7.cloned.1.call-start
  7.3 0.7 all-gather.7.cloned.1.call-update
  8.0 0.0 all-gather.9.cloned.1.call-start
  8.1 0.7 all-gather.9.cloned.1.call-update
  8.7 0.0 copy-start.3
  8.8 0.0 copy-start.2
  8.8 0.0 all-gather.11.cloned.1.call-start
  8.8 0.5 all-gather.11.cloned.1.call-update
  9.3 0.0 reduce-scatter.2.cloned.1.call-start
  9.4 0.0 copy-done.3
  9.4 0.0 copy-done
  9.4 1.9 gather_fusion.1
  11.4 0.0 copy-done.2
  11.4 0.1 fusion.15
  11.5 80.9 %all-gather.5.cloned.1.call-done = bf16[256,8192]{1,0:T(8,128)(2,1)} async-done(((bf16[64,8192]{1,0:T(8,128)(2,1)}), bf16[256,8192]{1,0:T(8,128)(2,1)}) %all-gather.5.cloned.1.call-update) | async-done | bytes 4194320 | tf_op jit(solution)/shard_map/all_gather | solution.py:17
  92.4 12.8 gather_fusion
  105.3 5.1 fusion
  110.3 370.8 %all-gather.7.cloned.1.call-done = bf16[8192,2048]{1,0:T(8,128)(2,1)} async-done(((bf16[4096,2048]{1,0:T(8,128)(2,1)}), bf16[8192,2048]{1,0:T(8,128)(2,1)}) %all-gather.7.cloned.1.call-update) | async-done | bytes 33554448 | tf_op jit(solution)/shard_map/all_gather | solution.py:23
  481.1 21.1 %fusion.13 = f32[256,2048]{1,0:T(8,128)S(1)} fusion(bf16[8192,2048]{1,0:T(8,128)(2,1)} %all-gather.7.cloned.1.call-done, f32[8192]{0:T(1024)S(1)} %bitcast.12, f32[8192]{0:T(1024)S(1)} %bitcast.10, f32[256]{0:T(256)S(1)} %add_rsqrt_fusion, pred[256]{0:T(512)(128)(4,1)S(1)} %get-tuple-element.5, bf16[256,8192]{1,0:T(8,128)(2,1)} %gather_fusion, ...), kind=kOutput, calls=%fused_computation.23 | convolution fusion | flops 8602517504 | bytes 39912960 | tf_op jit(solution)/shard_map/dot_general | solution.py:21
  502.2 369.1 %all-gather.9.cloned.1.call-done = bf16[8192,2048]{1,0:T(8,128)(2,1)} async-done(((bf16[4096,2048]{1,0:T(8,128)(2,1)}), bf16[8192,2048]{1,0:T(8,128)(2,1)}) %all-gather.9.cloned.1.call-update) | async-done | bytes 33554448 | tf_op jit(solution)/shard_map/all_gather | solution.py:28
  871.3 21.3 %fusion.3.clone.4 = bf16[256,2048]{1,0:T(8,128)(2,1)S(1)} fusion(bf16[8192,2048]{1,0:T(8,128)(2,1)} %all-gather.9.cloned.1.call-done, f32[256,2048]{1,0:T(8,128)S(1)} %fusion.13, f32[8192]{0:T(1024)S(1)} %bitcast.13, f32[8192]{0:T(1024)S(1)} %bitcast.11, f32[256]{0:T(256)S(1)} %add_rsqrt_fusion, pred[256]{0:T(512)(128)(4,1)S(1)} %get-tuple-element.5, ...), kind=kOutput, calls=%fused_computation.10.clone.clone.clone.1 | convolution fusion | flops 8605663232 | bytes 40961536 | tf_op jit(solution)/shard_map/dot_general | solution.py:26
  892.6 368.7 %all-gather.11.cloned.1.call-done = bf16[2048,8192]{1,0:T(8,128)(2,1)} async-done(((bf16[2048,4096]{1,0:T(8,128)(2,1)}), bf16[2048,8192]{1,0:T(8,128)(2,1)}) %all-gather.11.cloned.1.call-update) | async-done | bytes 33554448 | tf_op jit(solution)/shard_map/all_gather | solution.py:32
  1261.3 0.0 copy-start.1
  1261.3 16.4 %convolution_convert_fusion = bf16[256,8192]{1,0:T(8,128)(2,1)} fusion(bf16[2048,8192]{1,0:T(8,128)(2,1)} %all-gather.11.cloned.1.call-done, bf16[256,2048]{1,0:T(8,128)(2,1)S(1)} %fusion.3.clone.4), kind=kOutput, calls=%fused_computation.4 | convolution fusion | flops 8592031744 | bytes 38797312 | tf_op jit(solution)/shard_map/dot_general | solution.py:34
  1277.7 0.0 reduce-scatter.2.cloned.1.call-update
  1277.7 50.2 %reduce-scatter.2.cloned.1.call-done = bf16[32,8192]{1,0:T(8,128)(2,1)} async-done(((bf16[256,8192]{1,0:T(8,128)(2,1)}), bf16[32,8192]{1,0:T(8,128)(2,1)}) %reduce-scatter.2.cloned.1.call-update) | async-done | bytes 524304 | tf_op jit(solution)/shard_map/reduce_scatter | solution.py:33
  1327.8 0.0 copy-done.1
  (4 shorter events, 0.0 us)
Async XLA Ops:
  6.5 2.9 copy-start
  6.5 85.9 %all-gather.5.cloned.1.call-start = ((), (), s32[]{:S(2)}) async-start(), calls=%async_computation.1 | async-start | bytes 5242880 | tf_op jit(solution)/shard_map/all_gather | solution.py:17
  7.3 473.8 %all-gather.7.cloned.1.call-start = ((), (), s32[]{:S(2)}) async-start(), calls=%async_computation.2 | async-start | bytes 50331648 | tf_op jit(solution)/shard_map/all_gather | solution.py:23
  8.0 863.2 %all-gather.9.cloned.1.call-start = ((), (), s32[]{:S(2)}) async-start(), calls=%async_computation.3 | async-start | bytes 50331648 | tf_op jit(solution)/shard_map/all_gather | solution.py:28
  8.7 0.7 copy-start.3
  8.8 2.7 copy-start.2
  8.8 1252.5 %all-gather.11.cloned.1.call-start = ((), (), s32[]{:S(2)}) async-start(), calls=%async_computation.4 | async-start | bytes 50331648 | tf_op jit(solution)/shard_map/all_gather | solution.py:32
  9.3 1318.5 %reduce-scatter.2.cloned.1.call-start = ((), (), s32[]{:S(2)}) async-start(), calls=%async_computation.5 | async-start | bytes 4718592 | tf_op jit(solution)/shard_map/reduce_scatter | solution.py:33
  1261.3 66.6 %copy-start.1 = (s32[256]{0:T(256)S(1)}, s32[256]{0:T(256)}, u32[]{:S(2)}) copy-start(s32[256]{0:T(256)} %param.9) | copy-start | bytes 3076
Sparse Core Ops, SparseCore 0:
  8.9 83.4 all-gather.4
  94.0 387.0 all-gather.6
  482.7 388.5 all-gather.8
  872.7 388.5 all-gather.10
  1277.8 50.0 reduce-scatter.1
where the time goes:
time: 1330 us
  waiting for transfers between devices  1240 us (93%)
  matrix products  58.8 us (4%)
  local copies, waits for them, and re-layouts  14.9 us (1%)
    all_gather x1, waiting for transfers between devices, per_device(): lax.all_gather(gate_weight, 'dp', axis=0, tiled=True)  371 us
    all_gather x1, waiting for transfers between devices, per_device(): lax.all_gather(up_weight, 'dp', axis=0, tiled=True)  369 us
    all_gather x1, waiting for transfers between devices, per_device(): down_whole = lax.all_gather(down_weight, 'dp', axis=1, tiled=True)  369 us
    all_gather x1, waiting for transfers between devices, per_device(): whole_rows = lax.all_gather(tokens, 'tensor', axis=0, tiled=True)  80.9 us
    reduce_scatter x1, waiting for transfers between devices, per_device(): lax.psum_scatter(jnp.dot(hidden, down_whole, preferred_element_type=jnp.f...  50.2 us
  transfers between devices with their start and end apart: 5, of which 5 were waited for; matrix products, arithmetic and copies ran while one was open for 5% of the time, Pallas kernels for 0%

commit v1 on v0

v1 whole, which is shorter than its diff:
```python
import jax
import jax.numpy as jnp
from jax import lax
from jax.sharding import PartitionSpec as P

EPSILON = 1e-05


def normalize(block_rows, row_kinds, norm_gain):
    values = block_rows.astype(jnp.float32)
    inverse_rms = lax.rsqrt(jnp.mean(values * values, axis=1, keepdims=True) + EPSILON)
    chosen = jnp.where(row_kinds[:, None] == 1, norm_gain[1][None, :], norm_gain[0][None, :])
    return (values * inverse_rms * chosen).astype(jnp.bfloat16)


def exchange(pieces, n_dp):
    me = lax.axis_index("dp")
    got = jnp.zeros_like(pieces)
    got = lax.dynamic_update_index_in_dim(got, lax.dynamic_index_in_dim(pieces, me, 0, False), me, 0)
    for shift in range(1, n_dp):
        to = lax.rem(me + shift, n_dp)
        arrived = lax.ppermute(
            lax.dynamic_index_in_dim(pieces, to, 0, False),
            "dp",
            [(i, (i + shift) % n_dp) for i in range(n_dp)],
        )
        got = lax.dynamic_update_index_in_dim(got, arrived, lax.rem(me - shift + n_dp, n_dp), 0)
    return got


def spread(block, n_dp):
    me = lax.axis_index("dp")
    got = jnp.zeros((n_dp,) + block.shape, block.dtype)
    got = lax.dynamic_update_index_in_dim(got, block, me, 0)
    for shift in range(1, n_dp):
        arrived = lax.ppermute(block, "dp", [(i, (i + shift) % n_dp) for i in range(n_dp)])
        got = lax.dynamic_update_index_in_dim(got, arrived, lax.rem(me - shift + n_dp, n_dp), 0)
    return got


def plain(mesh, tokens, time_order, modality, norm_gain, gate_weight, up_weight, down_weight):
    n_dp, n_tensor, n_pair = mesh.shape["dp"], mesh.shape["tensor"], mesh.shape["pair"]
    held, width = tokens.shape
    rows = time_order.shape[0]
    depth, hidden_units = gate_weight.shape
    first = lax.axis_index("tensor") * held
    normed = normalize(tokens, lax.dynamic_slice_in_dim(modality, first, held, 0), norm_gain)
    by_part = normed.reshape(held, n_dp, depth).transpose(1, 0, 2)
    blocks = exchange(by_part, n_dp)
    every = lax.all_gather(blocks, "tensor", axis=1, tiled=True).reshape(n_dp * rows, depth)
    gate_part = jnp.dot(every, gate_weight, preferred_element_type=jnp.float32)
    up_part = jnp.dot(every, up_weight, preferred_element_type=jnp.float32)
    both = jnp.stack([gate_part, up_part]).reshape(2, n_dp, rows, hidden_units).transpose(1, 0, 2, 3)
    got = exchange(both.astype(jnp.bfloat16), n_dp).astype(jnp.float32)
    own = lax.axis_index("dp")
    mine = lax.dynamic_index_in_dim(both, own, 0, False)
    at = jnp.arange(n_dp)[:, None, None, None]
    summed = mine + jnp.sum(jnp.where(at == own, 0.0, got), axis=0)
    hidden = (jax.nn.silu(summed[0]) * summed[1]).astype(jnp.bfloat16)
    chosen = (time_order[:, None] == jnp.arange(rows)[None, :]).astype(jnp.bfloat16)
    hidden = jnp.dot(chosen, hidden, preferred_element_type=jnp.float32).astype(jnp.bfloat16)
    hidden = spread(hidden, n_dp).reshape(n_dp * rows, hidden_units)
    partial = jnp.dot(hidden, down_weight, preferred_element_type=jnp.float32).astype(jnp.bfloat16)
    partial = partial.reshape(n_dp, rows, -1)
    partial = lax.psum_scatter(partial, ("tensor", "pair"), scatter_dimension=1, tiled=True)
    return exchange(partial, n_dp).transpose(1, 0, 2).reshape(rows // (n_tensor * n_pair), width)


def solution(mesh):
    placed = (
        P(("groups", "dp", "tensor"), None),
        P(("groups", "dp")),
        P(("groups", "dp")),
        P(),
        P("dp", ("tensor", "pair")),
        P("dp", ("tensor", "pair")),
        P(("tensor", "pair"), "dp"),
    )

    def per_device(*arrays):
        return plain(mesh, *arrays)

    return jax.shard_map(
        per_device,
        mesh=mesh,
        in_specs=placed,
        out_specs=P(("groups", "dp", "tensor", "pair"), None),
        check_vma=False,
    )
```

time: 1330 us -> 295 us (0.22)
  waiting for transfers between devices: 1240 us -> 214 us
  matrix products: 58.8 us -> 37.1 us
    all_gather x4 -> x1, waiting for transfers between devices: 1190 us -> 82.2 us  [plain(): lax.all_gather(blocks, 'tensor', axis=1, tiled=True)]
    ppermute x0 -> x4, waiting for transfers between devices: none -> 83.2 us  [the longest x3 60.7 us: exchange(): lax.ppermute(lax.dynamic_index_in_dim(pieces, to, 0, False), 'dp', [(i, (...]
    dot_general x3 -> x4, matrix products: 58.8 us -> 37.1 us  [the longest x1 13.8 us: plain(): up_part = jnp.dot(every, up_weight, preferred_element_type=jnp.float32)]
    gather x2 -> x0, local copies, waits for them, and re-layouts: 14.8 us -> none  [the longest x1 12.8 us: per_device(): sorted_rows = jnp.take(whole_rows, time_order, axis=0)]
  transfers between devices with their start and end apart: 5 -> 6, of which waited for: 5 -> 6; matrix products, arithmetic and copies ran while one was open for 5% -> 1% of each run, Pallas kernels for 0% -> 0%
where the time goes in v1:
time: 295 us
  waiting for transfers between devices  214 us (73%)
  matrix products  37.1 us (13%)
  local copies, waits for them, and re-layouts  15.1 us (5%)
  between operations  13.7 us (5%)
  starting transfers between devices  7.84 us (3%)
  other arithmetic  6.62 us (2%)
    all_gather x1, waiting for transfers between devices, plain(): lax.all_gather(blocks, 'tensor', axis=1, tiled=True)  82.2 us
    ppermute x3, waiting for transfers between devices, exchange(): lax.ppermute(lax.dynamic_index_in_dim(pieces, to, 0, False), 'dp', [(i, (...  60.7 us
    reduce_scatter x1, waiting for transfers between devices, plain(): lax.psum_scatter(partial, ('tensor', 'pair'), scatter_dimension=1, tiled=...  49 us
    ppermute x1, waiting for transfers between devices, spread(): lax.ppermute(block, 'dp', [(i, (i + shift) % n_dp) for i in range(n_dp)])  22.6 us
    dot_general x1, matrix products, plain(): up_part = jnp.dot(every, up_weight, preferred_element_type=jnp.float32)  13.8 us
    dot_general x1, matrix products, plain(): gate_part = jnp.dot(every, gate_weight, preferred_element_type=jnp.float32)  11.7 us
    dot_general x1, matrix products, plain(): jnp.dot(hidden, down_weight, preferred_element_type=jnp.float32)  10.7 us
    ppermute x3, starting transfers between devices, exchange(): lax.ppermute(lax.dynamic_index_in_dim(pieces, to, 0, False), 'dp', [(i, (...  6.08 us
  transfers between devices with their start and end apart: 6, of which 6 were waited for; matrix products, arithmetic and copies ran while one was open for 1% of the time, Pallas kernels for 0%

profile of v1, /device:TPU:0, one launch (start us, length us, event | category | flops | bytes accessed | tf_op | source)
XLA Modules:
  0.0 294.8 jit_solution(15541341765485631949)
XLA Ops:
  6.5 1.0 fusion.23
  7.5 1.5 fusion.14
  9.1 0.8 dynamic-slice_compare_fusion
  9.8 1.6 fusion.16
  11.4 0.8 reshape.52
  12.2 2.7 constant_dynamic-slice_fusion
  15.0 0.6 copy.22
  15.6 3.0 %collective-permute-start = (bf16[64,4096]{1,0:T(8,128)(2,1)S(1)}, bf16[64,4096]{1,0:T(8,128)(2,1)S(1)}, u32[]{:S(2)}, u32[]{:S(2)}) collective-permute-start(bf16[64,4096]{1,0:T(8,128)(2,1)S(1)} %bitcast.70), channel_id=1, source_target_pairs={{0,2},{2,0},{1,3},{3,1},{4,6},{6,4},{5,7},{7,5},{8,10},{10,8},{9,1... | collective-permute-start | bytes 1572872 | tf_op jit(solution)/shard_map/ppermute | solution.py:22
  18.7 0.6 fusion.20
  19.3 11.2 %collective-permute-done = bf16[64,4096]{1,0:T(8,128)(2,1)S(1)} collective-permute-done((bf16[64,4096]{1,0:T(8,128)(2,1)S(1)}, bf16[64,4096]{1,0:T(8,128)(2,1)S(1)}, u32[]{:S(2)}, u32[]{:S(2)}) %collective-permute-start) | collective-permute-done | bytes 524320 | tf_op jit(solution)/shard_map/ppermute | solution.py:22
  30.6 1.0 copy-done
  31.8 82.2 %all-gather.2.cloned.1.call-done = bf16[2,256,4096]{2,1,0:T(8,128)(2,1)} async-done(((bf16[2,64,4096]{2,1,0:T(8,128)(2,1)}), bf16[2,256,4096]{2,1,0:T(8,128)(2,1)}) %all-gather.2.cloned.1.call-update) | async-done | bytes 4194320 | tf_op jit(solution)/shard_map/all_gather | solution.py:50
  114.0 13.8 %fusion.11 = f32[1,2,256,2048]{3,2,1,0:T(8,128)S(1)} fusion(bf16[2,256,4096]{2,1,0:T(8,128)(2,1)} %all-gather.2.cloned.1.call-done, bf16[4096,2048]{1,0:T(8,128)(2,1)} %param.12), kind=kOutput, calls=%fused_computation.14 | convolution fusion | flops 8589934592 | bytes 25165824 | tf_op jit(solution)/shard_map/dot_general | solution.py:52
  127.8 11.7 %fusion.8 = f32[1,2,256,2048]{3,2,1,0:T(8,128)S(1)} fusion(bf16[2,256,4096]{2,1,0:T(8,128)(2,1)S(1)} %copy-done.1, bf16[4096,2048]{1,0:T(8,128)(2,1)} %param.11), kind=kOutput, calls=%fused_computation.13 | convolution fusion | flops 8589934592 | bytes 25165824 | tf_op jit(solution)/shard_map/dot_general | solution.py:51
  139.5 0.7 fusion.4
  140.5 1.5 collective-permute-start.1
  142.1 0.5 broadcast_in_dim.90
  142.9 45.1 %collective-permute-done.1 = bf16[2,256,2048]{2,1,0:T(8,128)(2,1)S(1)} collective-permute-done((bf16[2,256,2048]{2,1,0:T(8,128)(2,1)S(1)}, bf16[2,256,2048]{2,1,0:T(8,128)(2,1)S(1)}, u32[]{:S(2)}, u32[]{:S(2)}) %collective-permute-start.1) | collective-permute-done | bytes 2097184 | tf_op jit(solution)/shard_map/ppermute | solution.py:22
  188.2 1.2 select_reduce_fusion
  189.5 0.8 fusion.7
  190.5 0.9 bitcast_dynamic-update-slice_fusion.3
  191.4 1.5 collective-permute-start.2
  193.0 22.6 %collective-permute-done.2 = bf16[256,2048]{1,0:T(8,128)(2,1)S(1)} collective-permute-done((bf16[256,2048]{1,0:T(8,128)(2,1)S(1)}, bf16[256,2048]{1,0:T(8,128)(2,1)S(1)}, u32[]{:S(2)}, u32[]{:S(2)}) %collective-permute-start.2) | collective-permute-done | bytes 1048608 | tf_op jit(solution)/shard_map/ppermute | solution.py:36
  215.7 10.7 %convolution_convert_fusion = bf16[512,4096]{1,0:T(8,128)(2,1)} fusion(bf16[512,2048]{1,0:T(8,128)(2,1)S(1)} %bitcast.68, bf16[2048,4096]{1,0:T(8,128)(2,1)S(1)} %bitcast.75), kind=kOutput, calls=%fused_computation.9 | convolution fusion | flops 8592031744 | bytes 23068672 | tf_op jit(solution)/shard_map/dot_general | solution.py:63
  226.4 49.0 %reduce-scatter.2.cloned.1.call-done = bf16[2,32,4096]{2,1,0:T(8,128)(2,1)} async-done(((bf16[2,256,4096]{2,1,0:T(8,128)(2,1)}), bf16[2,32,4096]{2,1,0:T(8,128)(2,1)}) %reduce-scatter.2.cloned.1.call-update) | async-done | bytes 524304 | tf_op jit(solution)/shard_map/reduce_scatter | solution.py:65
  275.5 1.1 dynamic-slice_bitcast_fusion.1
  276.5 1.5 collective-permute-start.3
  278.1 0.5 copy.13
  278.6 4.3 %collective-permute-done.3 = bf16[32,4096]{1,0:T(8,128)(2,1)S(1)} collective-permute-done((bf16[32,4096]{1,0:T(8,128)(2,1)S(1)}, bf16[32,4096]{1,0:T(8,128)(2,1)S(1)}, u32[]{:S(2)}, u32[]{:S(2)}) %collective-permute-start.3) | collective-permute-done | bytes 262176 | tf_op jit(solution)/shard_map/ppermute | solution.py:22
  283.0 0.5 copy.14
  283.5 3.3 %dynamic_update_slice.35 = bf16[2,32,4096]{2,0,1:T(2,128)(2,1)S(1)} dynamic-update-slice(bf16[2,32,4096]{2,0,1:T(2,128)(2,1)S(1)} %copy.13, bf16[1,32,4096]{2,0,1:T(2,128)(2,1)S(1)} %copy.14, s32[]{:T(128)S(6)} %select_n.41, s32[]{:T(128)} %constant.81.clone.1, s32[]{:T(128)} %constant.81.clone.1) | dynamic-update-slice | bytes 524292 | tf_op jit(solution)/shard_map/jit(dynamic_update_index_in_dim)/dynamic_update_slice | solution.py:27
  286.9 1.1 copy.17
  (28 shorter events, 1.6 us)
Async XLA Ops:
  6.5 107.4 %all-gather.2.cloned.1.call-start = ((), (), s32[]{:S(2)}) async-start(), calls=%async_computation.1 | async-start | bytes 5242880 | tf_op jit(solution)/shard_map/all_gather | solution.py:50
  15.6 14.9 %collective-permute-start = (bf16[64,4096]{1,0:T(8,128)(2,1)S(1)}, bf16[64,4096]{1,0:T(8,128)(2,1)S(1)}, u32[]{:S(2)}, u32[]{:S(2)}) collective-permute-start(bf16[64,4096]{1,0:T(8,128)(2,1)S(1)} %bitcast.70), channel_id=1, source_target_pairs={{0,2},{2,0},{1,3},{3,1},{4,6},{6,4},{5,7},{7,5},{8,10},{10,8},{9,1... | collective-permute-start | bytes 1572872 | tf_op jit(solution)/shard_map/ppermute | solution.py:22
  30.5 1.0 copy-start
  31.6 243.9 %reduce-scatter.2.cloned.1.call-start = ((), (), s32[]{:S(2)}) async-start(), calls=%async_computation.2 | async-start | bytes 4718592 | tf_op jit(solution)/shard_map/reduce_scatter | solution.py:65
  114.0 13.9 %copy-start.1 = (bf16[2,256,4096]{2,1,0:T(8,128)(2,1)S(1)}, bf16[2,256,4096]{2,1,0:T(8,128)(2,1)}, u32[]{:S(2)}) copy-start(bf16[2,256,4096]{2,1,0:T(8,128)(2,1)} %all-gather.2.cloned.1.call-done) | copy-start | bytes 12582916
  140.5 47.4 %collective-permute-start.1 = (bf16[2,256,2048]{2,1,0:T(8,128)(2,1)S(1)}, bf16[2,256,2048]{2,1,0:T(8,128)(2,1)S(1)}, u32[]{:S(2)}, u32[]{:S(2)}) collective-permute-start(bf16[2,256,2048]{2,1,0:T(8,128)(2,1)S(1)} %dynamic-slice_bitcast_fusion), channel_id=1, source_target_pairs={{0,2},{2,0},{1,3},{3,1},{4,6},{6,4},{5,7},{7,5},{8,10},{10,8},{9,1... | collective-permute-start | bytes 6291464 | tf_op jit(solution)/shard_map/ppermute | solution.py:22
  189.4 1.1 copy-start.2
  189.5 26.2 %slice-start = ((s8[16777216]{0:T(1024)(128)(4,1)}), s8[4194304]{0:T(1024)(128)(4,1)S(1)}, s32[]{:S(2)}) async-start(s8[16777216]{0:T(1024)(128)(4,1)} %bitcast.74), calls=%async_computation.3 | async-start | bytes 8388608
  189.5 26.2 %slice-start.1 = ((s8[16777216]{0:T(1024)(128)(4,1)}), s8[4194304]{0:T(1024)(128)(4,1)S(1)}, s32[]{:S(2)}) async-start(s8[16777216]{0:T(1024)(128)(4,1)} %bitcast.74), calls=%async_computation.4 | async-start | bytes 8388608
  189.5 26.2 %slice-start.2 = ((s8[16777216]{0:T(1024)(128)(4,1)}), s8[4194304]{0:T(1024)(128)(4,1)S(1)}, s32[]{:S(2)}) async-start(s8[16777216]{0:T(1024)(128)(4,1)} %bitcast.74), calls=%async_computation.5 | async-start | bytes 8388608
  190.5 25.2 %slice-start.3 = ((s8[16777216]{0:T(1024)(128)(4,1)}), s8[4194304]{0:T(1024)(128)(4,1)S(1)}, s32[]{:S(2)}) async-start(s8[16777216]{0:T(1024)(128)(4,1)} %bitcast.74), calls=%async_computation.6 | async-start | bytes 8388608
  191.4 24.1 %collective-permute-start.2 = (bf16[256,2048]{1,0:T(8,128)(2,1)S(1)}, bf16[256,2048]{1,0:T(8,128)(2,1)S(1)}, u32[]{:S(2)}, u32[]{:S(2)}) collective-permute-start(bf16[256,2048]{1,0:T(8,128)(2,1)S(1)} %get-tuple-element.12), channel_id=1, source_target_pairs={{0,2},{2,0},{1,3},{3,1},{4,6},{6,4},{5,7},{7,5},{8,10},{10,8},{9,1... | collective-permute-start | bytes 3145736 | tf_op jit(solution)/shard_map/ppermute | solution.py:36
  276.5 6.4 %collective-permute-start.3 = (bf16[32,4096]{1,0:T(8,128)(2,1)S(1)}, bf16[32,4096]{1,0:T(8,128)(2,1)S(1)}, u32[]{:S(2)}, u32[]{:S(2)}) collective-permute-start(bf16[32,4096]{1,0:T(8,128)(2,1)S(1)} %get-tuple-element.7), channel_id=1, source_target_pairs={{0,2},{2,0},{1,3},{3,1},{4,6},{6,4},{5,7},{7,5},{8,10},{10,8},{9,1... | collective-permute-start | bytes 786440 | tf_op jit(solution)/shard_map/ppermute | solution.py:22
Sparse Core Ops, SparseCore 0:
  31.7 82.2 all-gather.1
  226.5 48.8 reduce-scatter.1

commit v2 on v1

--- a/solution.py
+++ b/solution.py
@@ -1,9 +1,13 @@
 import jax
 import jax.numpy as jnp
 from jax import lax
+from jax.experimental import pallas as pl
+from jax.experimental.pallas import tpu as pltpu
 from jax.sharding import PartitionSpec as P
 
 EPSILON = 1e-05
+BF, F32 = jnp.bfloat16, jnp.float32
+MESH = pl.DeviceIdType.MESH
 
 
 def normalize(block_rows, row_kinds, norm_gain):
@@ -66,6 +70,340 @@
     return exchange(partial, n_dp).transpose(1, 0, 2).reshape(rows // (n_tensor * n_pair), width)
 
 
+def fused(mesh, tokens, time_order, modality, norm_gain, gate_weight, up_weight, down_weight):
+    n_z = mesh.shape["tensor"]
+    held, width = tokens.shape
+    rows = time_order.shape[0]
+    depth, units = gate_weight.shape
+    out_w = down_weight.shape[1]
+    quarter = depth // 2
+    wide = 256
+    n_half = units // 2 // wide
+    span = 512
+    n_out = out_w // span
+    half_rows = rows // 2
+    share = half_rows // n_z
+
+    def kernel(tok, kinds, order, gain, gw, uw, dw, out,
+               xs, xg, order2, wgb, wdb, ps, pr, own, hid, sh, qs, qr, keep, zs, zr, acc, fs, fr,
+               wsem, dsem, xs_s, xs_r, o_s, o_r, ag_s, ag_rz, ag_rp, p_s, p_r, h_s, h_r,
+               q_s, q_r, z_s, z_r, f_s, f_r):
+        x, z, c = lax.axis_index("dp"), lax.axis_index("tensor"), lax.axis_index("pair")
+        ox, oc = 1 - x, 1 - c
+
+        def remote(src, dst, send, recv, **to):
+            return pltpu.make_async_remote_copy(
+                src_ref=src, dst_ref=dst, send_sem=send, recv_sem=recv, device_id=to, device_id_type=MESH)
+
+        def gu_copies(j, slot):
+            col = pl.multiple_of(lax.rem(ox * n_half + j, 2 * n_half) * wide, wide)
+            return (pltpu.make_async_copy(gw.at[:, pl.ds(col, wide)], wgb.at[slot, 0], wsem.at[slot, 0]),
+                    pltpu.make_async_copy(uw.at[:, pl.ds(col, wide)], wgb.at[slot, 1], wsem.at[slot, 1]))
+
+        def gu_start(j, slot):
+            for copy in gu_copies(j, slot):
+                copy.start()
+
+        def down_copy(n, slot):
+            col = pl.multiple_of(n * span, span)
+            return pltpu.make_async_copy(dw.at[:, pl.ds(col, span)], wdb.at[slot], dsem.at[slot])
+
+        gu_start(0, 0)
+        down_copy(0, 0).start()
+
+        barrier = pltpu.get_barrier_semaphore()
+        pl.semaphore_signal(barrier, inc=1, device_id={"dp": ox}, device_id_type=MESH)
+        pl.semaphore_signal(barrier, inc=1, device_id={"pair": oc}, device_id_type=MESH)
+        for o in range(1, n_z):
+            pl.semaphore_signal(barrier, inc=1, device_id={"tensor": lax.rem(z + o, n_z)}, device_id_type=MESH)
+
+        def norm_step(i, _):
+            at = pl.ds(pl.multiple_of(i * 16, 16), 16)
+            values = tok[at, :].astype(F32)
+            inverse = lax.rsqrt(jnp.mean(values * values, axis=1, keepdims=True) + EPSILON)
+            kind = kinds[at, 0:1]
+
+            def piece(first):
+                cols = pl.ds(pl.multiple_of(first, quarter), quarter)
+                chosen = jnp.where(kind == 1, gain[1:2, cols], gain[0:1, cols])
+                return (tok[at, cols].astype(F32) * inverse * chosen).astype(BF)
+
+            xs[at, :] = piece(ox * depth + c * quarter)
+            place = pl.ds(pl.multiple_of(z * held + i * 16, 16), 16)
+            for q in range(2):
+                xg[x, q, place, :] = piece(x * depth + q * quarter)
+            return 0
+
+        lax.fori_loop(0, held // 16, norm_step, 0)
+        pl.semaphore_wait(barrier, n_z + 1)
+
+        def zrows(o):
+            return pl.ds(pl.multiple_of(o * held, held), held)
+
+        x_copy = remote(xs, xg.at[x, c, zrows(z)], xs_s, xs_r, dp=ox)
+        x_copy.start()
+        o_copy = remote(order, order2, o_s, o_r, dp=ox)
+        o_copy.start()
+
+        def ag(b, o, way):
+            piece = xg.at[b, c, zrows(o)]
+            if way == 2:
+                return remote(piece, piece, ag_s.at[b, o, 2], ag_rp.at[b, o], pair=oc)
+            to = lax.rem(z + (1 if way == 0 else n_z - 1), n_z)
+            return remote(piece, piece, ag_s.at[b, o, way], ag_rz.at[b, o], tensor=to)
+
+        def ag_each(b, d, act):
+            if d == 0:
+                pl.when(z < n_z - 1)(lambda: act(ag(b, z, 0)))
+                pl.when(z > 0)(lambda: act(ag(b, z, 1)))
+                pl.when(x != b)(lambda: act(ag(b, z, 2)))
+                return
+            left, right = lax.rem(z - d + n_z, n_z), lax.rem(z + d, n_z)
+            pl.when((z >= d) & (z < n_z - 1))(lambda: act(ag(b, left, 0)))
+            pl.when(z >= d)(lambda: act(ag(b, left, 2)))
+            pl.when((z + d < n_z) & (z > 0))(lambda: act(ag(b, right, 1)))
+            pl.when(z + d < n_z)(lambda: act(ag(b, right, 2)))
+
+        def begin(copy):
+            copy.start()
+
+        def sent(copy):
+            copy.wait_send()
+
+        def own_sends(b):
+            @pl.when(x != b)
+            def _():
+                remote(xs, xg.at[b, c, zrows(z)], xs_s, xs_r, dp=ox).wait_recv()
+            ag_each(b, 0, begin)
+
+        def hops(b):
+            for d in range(1, n_z):
+                left, right = lax.rem(z - d + n_z, n_z), lax.rem(z + d, n_z)
+                pl.when(z >= d)(lambda: ag(b, left, 0).wait_recv())
+                pl.when(z + d < n_z)(lambda: ag(b, right, 1).wait_recv())
+                ag_each(b, d, begin)
+
+        def sibling(b, o):
+            piece = xg.at[b, oc, zrows(o)]
+            remote(piece, piece, ag_s.at[b, o, 2], ag_rp.at[b, o], pair=oc).wait_recv()
+
+        def siblings(b):
+            pl.when(x != b)(lambda: sibling(b, z))
+            for d in range(1, n_z):
+                sibling(b, lax.rem(z + d, n_z))
+
+        def p_copy(b, j):
+            return remote(ps.at[b, j], pr.at[b, j], p_s.at[b, j], p_r.at[b, j], dp=ox)
+
+        def gate_up(b):
+            def step(j, _):
+                slot = lax.rem(j, 2)
+                if b == 0:
+                    gu_start(lax.rem(j + 1, 2 * n_half), 1 - slot)
+                else:
+                    pl.when(j + 1 < 2 * n_half)(lambda: gu_start(j + 1, 1 - slot))
+                for copy in gu_copies(j, slot):
+                    copy.wait()
+                got = []
+                for m in range(2):
+                    got.append(jnp.dot(xg[b, 0], wgb[slot, m, :quarter, :], preferred_element_type=F32)
+                               + jnp.dot(xg[b, 1], wgb[slot, m, quarter:, :], preferred_element_type=F32))
+
+                @pl.when(j < n_half)
+                def _():
+                    ps[b, j, 0] = got[0].astype(BF)
+                    ps[b, j, 1] = got[1].astype(BF)
+                    p_copy(b, j).start()
+
+                @pl.when(j >= n_half)
+                def _():
+                    own[b, lax.rem(j, n_half), 0] = got[0]
+                    own[b, lax.rem(j, n_half), 1] = got[1]
+                return 0
+            lax.fori_loop(0, 2 * n_half, step, 0)
+
+        def h_copy(b, j, half):
+            piece = hid.at[b, half * n_half + j]
+            return remote(piece, piece, h_s.at[b, j], h_r.at[b, j], dp=ox)
+
+        def hidden(b):
+            def step(j, _):
+                p_copy(b, j).wait_recv()
+                gate = own[b, j, 0] + pr[b, j, 0].astype(F32)
+                up = own[b, j, 1] + pr[b, j, 1].astype(F32)
+                hid[b, x * n_half + j] = (gate / (1.0 + jnp.exp(-gate)) * up).astype(BF)
+                h_copy(b, j, x).start()
+                return 0
+            lax.fori_loop(0, n_half, step, 0)
+
+        def sort(b):
+            at = jnp.where(x == b, order[...], order2[...])[0:1, :]
+            match = (lax.broadcasted_iota(jnp.int32, (rows, rows), 0) == at).astype(F32)
+            chosen = jnp.transpose(match).astype(BF)
+
+            def step(j, _):
+                h_copy(b, j, ox).wait_recv()
+                return 0
+            lax.fori_loop(0, n_half, step, 0)
+            for k in range(2 * n_half):
+                sh[:, k * wide:(k + 1) * wide] = jnp.dot(
+                    chosen, hid[b, k], preferred_element_type=F32).astype(BF)
+
+        def q_copy(b, n):
+            return remote(qs.at[b, n], qr.at[b, n], q_s.at[b, n], q_r.at[b, n], pair=oc)
+
+        def z_copy(b, n, o):
+            to = lax.rem(z + o, n_z)
+            return remote(zs.at[b, n, pl.ds(pl.multiple_of(to * share, share), share)], zr.at[b, n, z],
+                          z_s.at[b, n, o], z_r.at[b, n, z], tensor=to)
+
+        def z_arrival(b, n, o):
+            src = lax.rem(z + o, n_z)
+            return remote(zs.at[b, n, pl.ds(0, share)], zr.at[b, n, src],
+                          z_s.at[b, n, o], z_r.at[b, n, src], tensor=src)
+
+        def reduce(b, n):
+            slot = lax.rem(n, 2)
+            q_copy(b, n).wait_recv()
+            total = keep[slot] + qr[b, n].astype(F32)
+            zs[b, n] = total.astype(BF)
+            for o in range(1, n_z):
+                z_copy(b, n, o).start()
+            keep[slot] = total
+            acc[b, n] = keep[slot, pl.ds(pl.multiple_of(z * share, share), share), :]
+
+        def down(b):
+            def step(n, _):
+                slot = lax.rem(n, 2)
+                if b == 0:
+                    down_copy(lax.rem(n + 1, n_out), 1 - slot).start()
+                else:
+                    pl.when(n + 1 < n_out)(lambda: down_copy(n + 1, 1 - slot).start())
+                down_copy(n, slot).wait()
+                part = jnp.dot(sh[...], wdb[slot], preferred_element_type=F32)
+                qs[b, n] = part[half_rows:].astype(BF)
+                q_copy(b, n).start()
+                keep[slot] = part[:half_rows]
+                pl.when(n >= 1)(lambda: reduce(b, n - 1))
+                return 0
+            lax.fori_loop(0, n_out, step, 0)
+            reduce(b, n_out - 1)
+
+        def f_copy(n):
+            return remote(fs.at[n], fr.at[n], f_s.at[n], f_r.at[n], dp=ox)
+
+        def finish(b):
+            def step(n, _):
+                total = acc[b, n]
+                for o in range(1, n_z):
+                    z_arrival(b, n, o).wait_recv()
+                    total = total + zr[b, n, lax.rem(z + o, n_z)].astype(F32)
+
+                @pl.when(x == b)
+                def _():
+                    out[:, pl.ds(pl.multiple_of(b * out_w + n * span, span), span)] = total.astype(BF)
+
+                @pl.when(x != b)
+                def _():
+                    fs[n] = total.astype(BF)
+                    f_copy(n).start()
+                return 0
+            lax.fori_loop(0, n_out, step, 0)
+
+        own_sends(0)
+        hops(0)
+        own_sends(1)
+        siblings(0)
+        gate_up(0)
+        hops(1)
+        siblings(1)
+        gate_up(1)
+        hidden(0)
+        o_copy.wait_recv()
+        sort(0)
+        down(0)
+        hidden(1)
+        sort(1)
+        down(1)
+        finish(0)
+        finish(1)
+
+        def last(n, _):
+            f_copy(n).wait_recv()
+            out[:, pl.ds(pl.multiple_of(ox * out_w + n * span, span), span)] = fr[n]
+            return 0
+        lax.fori_loop(0, n_out, last, 0)
+
+        x_copy.wait_send()
+        o_copy.wait_send()
+        for b in range(2):
+            for d in range(n_z):
+                ag_each(b, d, sent)
+
+            def sent_x(j, _):
+                p_copy(b, j).wait_send()
+                h_copy(b, j, x).wait_send()
+                return 0
+            lax.fori_loop(0, n_half, sent_x, 0)
+
+            def sent_z(n, _):
+                q_copy(b, n).wait_send()
+                for o in range(1, n_z):
+                    z_copy(b, n, o).wait_send()
+                return 0
+            lax.fori_loop(0, n_out, sent_z, 0)
+
+        def sent_f(n, _):
+            f_copy(n).wait_send()
+            return 0
+        lax.fori_loop(0, n_out, sent_f, 0)
+
+    z, c = lax.axis_index("tensor"), lax.axis_index("pair")
+    kinds = lax.dynamic_slice_in_dim(modality, z * held, held, 0)
+    kinds = jnp.broadcast_to(kinds[:, None], (held, 128))
+    order = time_order.reshape(n_z, 2, share).transpose(1, 0, 2)
+    order = jnp.where(c == 0, order, order[::-1]).reshape(1, rows)
+    order = jnp.broadcast_to(order, (8, rows))
+    vmem, anywhere = pl.BlockSpec(memory_space=pltpu.VMEM), pl.BlockSpec(memory_space=pl.ANY)
+    dma = pltpu.SemaphoreType.DMA
+    scratch = [
+        pltpu.VMEM((held, quarter), BF),
+        pltpu.VMEM((2, 2, rows, quarter), BF),
+        pltpu.VMEM((8, rows), jnp.int32),
+        pltpu.VMEM((2, 2, depth, wide), BF),
+        pltpu.VMEM((2, units, span), BF),
+        pltpu.VMEM((2, n_half, 2, rows, wide), BF),
+        pltpu.VMEM((2, n_half, 2, rows, wide), BF),
+        pltpu.VMEM((2, n_half, 2, rows, wide), F32),
+        pltpu.VMEM((2, 2 * n_half, rows, wide), BF),
+        pltpu.VMEM((rows, units), BF),
+        pltpu.VMEM((2, n_out, half_rows, span), BF),
+        pltpu.VMEM((2, n_out, half_rows, span), BF),
+        pltpu.VMEM((2, half_rows, span), F32),
+        pltpu.VMEM((2, n_out, half_rows, span), BF),
+        pltpu.VMEM((2, n_out, n_z, share, span), BF),
+        pltpu.VMEM((2, n_out, share, span), F32),
+        pltpu.VMEM((n_out, share, span), BF),
+        pltpu.VMEM((n_out, share, span), BF),
+        dma((2, 2)), dma((2,)), dma, dma, dma, dma,
+        dma((2, n_z, 3)), dma((2, n_z)), dma((2, n_z)),
+        dma((2, n_half)), dma((2, n_half)), dma((2, n_half)), dma((2, n_half)),
+        dma((2, n_out)), dma((2, n_out)), dma((2, n_out, n_z)), dma((2, n_out, n_z)),
+        dma((n_out,)), dma((n_out,)),
+    ]
+    return pl.pallas_call(
+        kernel,
+        out_shape=jax.ShapeDtypeStruct((rows // (n_z * 2), width), BF),
+        in_specs=[vmem, vmem, vmem, vmem, anywhere, anywhere, anywhere],
+        out_specs=vmem,
+        scratch_shapes=scratch,
+        compiler_params=pltpu.CompilerParams(
+            collective_id=0, has_side_effects=True, vmem_limit_bytes=58 * 2**20),
+        cost_estimate=pl.CostEstimate(
+            flops=12 * rows * depth * units, bytes_accessed=12 * depth * units, transcendentals=0),
+    )(tokens, kinds, order, norm_gain, gate_weight, up_weight, down_weight)
+
+
 def solution(mesh):
     placed = (
         P(("groups", "dp", "tensor"), None),
@@ -78,6 +416,9 @@
     )
 
     def per_device(*arrays):
+        share = arrays[1].shape[0] // (mesh.shape["tensor"] * mesh.shape["pair"])
+        if mesh.shape["dp"] == 2 and mesh.shape["pair"] == 2 and share % 16 == 0:
+            return fused(mesh, *arrays)
         return plain(mesh, *arrays)
 
     return jax.shard_map(

time: 295 us -> 147 us (0.50)
  waiting for transfers between devices: 214 us -> 0 us
  Pallas kernels: 0 us -> 142 us
  matrix products: 37.1 us -> 0 us
  between operations: 13.7 us -> 0.02 us
  local copies, waits for them, and re-layouts: 15.1 us -> 4.78 us
  starting transfers between devices: 7.84 us -> 0 us
  other arithmetic: 6.62 us -> 0.01 us
    pallas_call x0 -> x1, Pallas kernels: none -> 142 us  [fused(): pl.pallas_call(kernel, out_shape=jax.ShapeDtypeStruct((rows // (n_z * 2),...]
    ppermute x4 -> x0, waiting for transfers between devices: 83.2 us -> none  [the longest x3 60.7 us: exchange(): lax.ppermute(lax.dynamic_index_in_dim(pieces, to, 0, False), 'dp', [(i, (...]
    all_gather x1 -> x0, waiting for transfers between devices: 82.2 us -> none  [plain(): lax.all_gather(blocks, 'tensor', axis=1, tiled=True)]
    reduce_scatter x1 -> x0, waiting for transfers between devices: 49 us -> none  [plain(): lax.psum_scatter(partial, ('tensor', 'pair'), scatter_dimension=1, tiled=...]
    dot_general x4 -> x0, matrix products: 37.1 us -> none  [the longest x1 13.8 us: plain(): up_part = jnp.dot(every, up_weight, preferred_element_type=jnp.float32)]
    ppermute x4 -> x0, starting transfers between devices: 7.61 us -> none  [the longest x3 6.08 us: exchange(): lax.ppermute(lax.dynamic_index_in_dim(pieces, to, 0, False), 'dp', [(i, (...]
    dynamic_update_slice x7 -> x0, local copies, waits for them, and re-layouts: 5.18 us -> none  [the longest x3 3.63 us: exchange(): lax.dynamic_update_index_in_dim(got, arrived, lax.rem(me - shift + n_dp,...]
  transfers between devices with their start and end apart: 6 -> 0, of which waited for: 6 -> 0; matrix products, arithmetic and copies ran while one was open for 1% -> 0% of each run, Pallas kernels for 0% -> 0%
where the time goes in v2:
time: 147 us
  Pallas kernels  142 us (97%)
  local copies, waits for them, and re-layouts  4.78 us (3%)
    pallas_call x1, Pallas kernels, fused(): pl.pallas_call(kernel, out_shape=jax.ShapeDtypeStruct((rows // (n_z * 2),...  142 us

profile of v2, /device:TPU:0, one launch (start us, length us, event | category | flops | bytes accessed | tf_op | source)
XLA Modules:
  0.0 146.6 jit_solution(1479246321905268834)
XLA Ops:
  0.0 0.8 dynamic_slice.3
  0.8 0.8 reshape.6
  1.6 0.1 broadcast_in_dim.14
  1.6 0.6 broadcast_in_dim.15.order
  2.2 0.7 broadcast_in_dim.6.kinds
  2.9 141.8 %shard_map.73 = bf16[32,8192]{1,0:T(8,128)(2,1)} custom-call(bf16[64,8192]{1,0:T(8,128)(2,1)} %tok.1, s32[64,128]{1,0:T(8,128)} %broadcast_in_dim.6.kinds, s32[8,256]{1,0:T(8,128)} %broadcast_in_dim.15.order, f32[2,8192]{1,0:T(2,128)} %gain.1, bf16[4096,2048]{1,0:T(8,128)(2,1)} %gw.1, bf16[4096,2048]{1,0:T(8,128)(2,1)} %uw.1, bf16[2048,4096]{1,0:T(8,128)(2,1)} %dw.1), custom_call_target="tpu_custom_call" | custom-call | flops 25769803776 | bytes 100663296 | tf_op jit(solution)/shard_map/pallas_call | solution.py:394
  144.7 1.9 %copy.10 = bf16[32,8192]{1,0:T(8,128)(2,1)} copy(bf16[32,8192]{1,0:T(8,128)(2,1)} %shard_map.73) | data formatting | bytes 1048576
  (3 shorter events, 0.0 us)

commit v3 on v2

--- a/solution.py
+++ b/solution.py
@@ -82,10 +82,12 @@
     span = 512
     n_out = out_w // span
     half_rows = rows // 2
-    share = half_rows // n_z
+    near = n_z // 2
+    kept = half_rows // 2
+    share = kept // n_z
 
     def kernel(tok, kinds, order, gain, gw, uw, dw, out,
-               xs, xg, order2, wgb, wdb, ps, pr, own, hid, sh, qs, qr, keep, zs, zr, acc, fs, fr,
+               xs, xg, xt, order2, wgb, wdb, ps, pr, own, hid, sh, qs, qr, keep, zs, zr, acc, fs, fr,
                wsem, dsem, xs_s, xs_r, o_s, o_r, ag_s, ag_rz, ag_rp, p_s, p_r, h_s, h_r,
                q_s, q_r, z_s, z_r, f_s, f_r):
         x, z, c = lax.axis_index("dp"), lax.axis_index("tensor"), lax.axis_index("pair")
@@ -176,163 +178,214 @@
                 remote(xs, xg.at[b, c, zrows(z)], xs_s, xs_r, dp=ox).wait_recv()
             ag_each(b, 0, begin)
 
-        def hops(b):
-            for d in range(1, n_z):
-                left, right = lax.rem(z - d + n_z, n_z), lax.rem(z + d, n_z)
-                pl.when(z >= d)(lambda: ag(b, left, 0).wait_recv())
-                pl.when(z + d < n_z)(lambda: ag(b, right, 1).wait_recv())
-                ag_each(b, d, begin)
+        def hop(b, d):
+            left, right = lax.rem(z - d + n_z, n_z), lax.rem(z + d, n_z)
+            pl.when(z >= d)(lambda: ag(b, left, 0).wait_recv())
+            pl.when(z + d < n_z)(lambda: ag(b, right, 1).wait_recv())
+            ag_each(b, d, begin)
 
         def sibling(b, o):
             piece = xg.at[b, oc, zrows(o)]
             remote(piece, piece, ag_s.at[b, o, 2], ag_rp.at[b, o], pair=oc).wait_recv()
 
-        def siblings(b):
-            pl.when(x != b)(lambda: sibling(b, z))
-            for d in range(1, n_z):
-                sibling(b, lax.rem(z + d, n_z))
-
-        def p_copy(b, j):
-            return remote(ps.at[b, j], pr.at[b, j], p_s.at[b, j], p_r.at[b, j], dp=ox)
-
-        def gate_up(b):
+        def siblings(b, half):
+            for k in range(near):
+                o = half * near + k
+                pl.when((x != b) | (o != z))(lambda: sibling(b, o))
+
+        def p_copy(u, j):
+            return remote(ps.at[u, j], pr.at[u, j], p_s.at[u, j], p_r.at[u, j], dp=ox)
+
+        def gate_up(u, rows_of, part, final=False):
             def step(j, _):
                 slot = lax.rem(j, 2)
-                if b == 0:
+                if final:
+                    pl.when(j + 1 < 2 * n_half)(lambda: gu_start(j + 1, 1 - slot))
+                else:
                     gu_start(lax.rem(j + 1, 2 * n_half), 1 - slot)
-                else:
-                    pl.when(j + 1 < 2 * n_half)(lambda: gu_start(j + 1, 1 - slot))
                 for copy in gu_copies(j, slot):
                     copy.wait()
-                got = []
                 for m in range(2):
-                    got.append(jnp.dot(xg[b, 0], wgb[slot, m, :quarter, :], preferred_element_type=F32)
-                               + jnp.dot(xg[b, 1], wgb[slot, m, quarter:, :], preferred_element_type=F32))
-
-                @pl.when(j < n_half)
-                def _():
-                    ps[b, j, 0] = got[0].astype(BF)
-                    ps[b, j, 1] = got[1].astype(BF)
-                    p_copy(b, j).start()
-
-                @pl.when(j >= n_half)
-                def _():
-                    own[b, lax.rem(j, n_half), 0] = got[0]
-                    own[b, lax.rem(j, n_half), 1] = got[1]
-                return 0
-            lax.fori_loop(0, 2 * n_half, step, 0)
-
-        def h_copy(b, j, half):
-            piece = hid.at[b, half * n_half + j]
-            return remote(piece, piece, h_s.at[b, j], h_r.at[b, j], dp=ox)
-
-        def hidden(b):
+                    got = (jnp.dot(rows_of(0), wgb[slot, m, :quarter, :], preferred_element_type=F32)
+                           + jnp.dot(rows_of(1), wgb[slot, m, quarter:, :], preferred_element_type=F32))
+                    if part == 0:
+                        ps[u, j, m] = got.astype(BF)
+                    else:
+                        own[u, j - n_half, m] = got
+                if part == 0:
+                    p_copy(u, j).start()
+                return 0
+            lax.fori_loop(part * n_half, (part + 1) * n_half, step, 0)
+
+        def arrived(half):
+            at = pl.ds(pl.multiple_of(half * half_rows, half_rows), half_rows)
+            return lambda q: xg[0, q, at, :]
+
+        def h_copy(u, j, half):
+            piece = hid.at[u, half * n_half + j]
+            return remote(piece, piece, h_s.at[u, j], h_r.at[u, j], dp=ox)
+
+        def hidden(u):
             def step(j, _):
-                p_copy(b, j).wait_recv()
-                gate = own[b, j, 0] + pr[b, j, 0].astype(F32)
-                up = own[b, j, 1] + pr[b, j, 1].astype(F32)
-                hid[b, x * n_half + j] = (gate / (1.0 + jnp.exp(-gate)) * up).astype(BF)
-                h_copy(b, j, x).start()
+                p_copy(u, j).wait_recv()
+                gate = own[u, j, 0] + pr[u, j, 0].astype(F32)
+                up = own[u, j, 1] + pr[u, j, 1].astype(F32)
+                hid[u, x * n_half + j] = (gate / (1.0 + jnp.exp(-gate)) * up).astype(BF)
+                h_copy(u, j, x).start()
                 return 0
             lax.fori_loop(0, n_half, step, 0)
 
-        def sort(b):
+        def hidden_arrival(u):
+            def step(j, _):
+                h_copy(u, j, ox).wait_recv()
+                return 0
+            lax.fori_loop(0, n_half, step, 0)
+
+        def chooser(b):
             at = jnp.where(x == b, order[...], order2[...])[0:1, :]
             match = (lax.broadcasted_iota(jnp.int32, (rows, rows), 0) == at).astype(F32)
-            chosen = jnp.transpose(match).astype(BF)
-
-            def step(j, _):
-                h_copy(b, j, ox).wait_recv()
-                return 0
-            lax.fori_loop(0, n_half, step, 0)
+            return jnp.transpose(match).astype(BF)
+
+        def sort_hidden():
+            chosen = chooser(0)
             for k in range(2 * n_half):
-                sh[:, k * wide:(k + 1) * wide] = jnp.dot(
-                    chosen, hid[b, k], preferred_element_type=F32).astype(BF)
-
-        def q_copy(b, n):
-            return remote(qs.at[b, n], qr.at[b, n], q_s.at[b, n], q_r.at[b, n], pair=oc)
-
-        def z_copy(b, n, o):
+                sh[:, k * wide:(k + 1) * wide] = (
+                    jnp.dot(chosen[:, :half_rows], hid[0, k], preferred_element_type=F32)
+                    + jnp.dot(chosen[:, half_rows:], hid[1, k], preferred_element_type=F32)).astype(BF)
+
+        def sort_tokens():
+            chosen = chooser(1)
+            for q in range(2):
+                for k in range(0, quarter, span):
+                    moved = jnp.dot(chosen, xg[1, q, :, k:k + span], preferred_element_type=F32).astype(BF)
+                    xt[0, q, :, k:k + span] = moved[:half_rows]
+                    xt[1, q, :, k:k + span] = moved[half_rows:]
+
+        def in_order(u):
+            for k in range(2 * n_half):
+                sh[:half_rows, k * wide:(k + 1) * wide] = hid[u, k]
+
+        def q_copy(u, n):
+            return remote(qs.at[u, n], qr.at[u, n], q_s.at[u, n], q_r.at[u, n], pair=oc)
+
+        def z_copy(u, n, o):
             to = lax.rem(z + o, n_z)
-            return remote(zs.at[b, n, pl.ds(pl.multiple_of(to * share, share), share)], zr.at[b, n, z],
-                          z_s.at[b, n, o], z_r.at[b, n, z], tensor=to)
-
-        def z_arrival(b, n, o):
+            return remote(zs.at[u, n, pl.ds(pl.multiple_of(to * share, share), share)], zr.at[u, n, z],
+                          z_s.at[u, n, o], z_r.at[u, n, z], tensor=to)
+
+        def z_arrival(u, n, o):
             src = lax.rem(z + o, n_z)
-            return remote(zs.at[b, n, pl.ds(0, share)], zr.at[b, n, src],
-                          z_s.at[b, n, o], z_r.at[b, n, src], tensor=src)
-
-        def reduce(b, n):
+            return remote(zs.at[u, n, pl.ds(0, share)], zr.at[u, n, src],
+                          z_s.at[u, n, o], z_r.at[u, n, src], tensor=src)
+
+        def reduce(units_of, n):
             slot = lax.rem(n, 2)
-            q_copy(b, n).wait_recv()
-            total = keep[slot] + qr[b, n].astype(F32)
-            zs[b, n] = total.astype(BF)
-            for o in range(1, n_z):
-                z_copy(b, n, o).start()
-            keep[slot] = total
-            acc[b, n] = keep[slot, pl.ds(pl.multiple_of(z * share, share), share), :]
-
-        def down(b):
+            for i, u in enumerate(units_of):
+                q_copy(u, n).wait_recv()
+                total = keep[slot, i] + qr[u, n].astype(F32)
+                zs[u, n] = total.astype(BF)
+                for o in range(1, n_z):
+                    z_copy(u, n, o).start()
+                keep[slot, i] = total
+                acc[u, n] = keep[slot, i, pl.ds(pl.multiple_of(z * share, share), share), :]
+
+        def down(units_of, final=False):
+            many = len(units_of)
+
             def step(n, _):
                 slot = lax.rem(n, 2)
-                if b == 0:
+                if final:
+                    pl.when(n + 1 < n_out)(lambda: down_copy(n + 1, 1 - slot).start())
+                else:
                     down_copy(lax.rem(n + 1, n_out), 1 - slot).start()
-                else:
-                    pl.when(n + 1 < n_out)(lambda: down_copy(n + 1, 1 - slot).start())
                 down_copy(n, slot).wait()
-                part = jnp.dot(sh[...], wdb[slot], preferred_element_type=F32)
-                qs[b, n] = part[half_rows:].astype(BF)
-                q_copy(b, n).start()
-                keep[slot] = part[:half_rows]
-                pl.when(n >= 1)(lambda: reduce(b, n - 1))
+                part = jnp.dot(sh[:many * half_rows, :], wdb[slot], preferred_element_type=F32)
+                for i, u in enumerate(units_of):
+                    qs[u, n] = part[i * half_rows + kept:(i + 1) * half_rows].astype(BF)
+                    q_copy(u, n).start()
+                    keep[slot, i] = part[i * half_rows:i * half_rows + kept]
+                pl.when(n >= 1)(lambda: reduce(units_of, n - 1))
                 return 0
             lax.fori_loop(0, n_out, step, 0)
-            reduce(b, n_out - 1)
-
-        def f_copy(n):
-            return remote(fs.at[n], fr.at[n], f_s.at[n], f_r.at[n], dp=ox)
-
-        def finish(b):
+            reduce(units_of, n_out - 1)
+
+        def f_copy(h, n):
+            return remote(fs.at[h, n], fr.at[h, n], f_s.at[h, n], f_r.at[h, n], dp=ox)
+
+        def finish(u):
+            b, h = u // 2, u % 2
+
             def step(n, _):
-                total = acc[b, n]
+                total = acc[u, n]
                 for o in range(1, n_z):
-                    z_arrival(b, n, o).wait_recv()
-                    total = total + zr[b, n, lax.rem(z + o, n_z)].astype(F32)
+                    z_arrival(u, n, o).wait_recv()
+                    total = total + zr[u, n, lax.rem(z + o, n_z)].astype(F32)
 
                 @pl.when(x == b)
                 def _():
-                    out[:, pl.ds(pl.multiple_of(b * out_w + n * span, span), span)] = total.astype(BF)
+                    out[h * share:(h + 1) * share,
+                        pl.ds(pl.multiple_of(b * out_w + n * span, span), span)] = total.astype(BF)
 
                 @pl.when(x != b)
                 def _():
-                    fs[n] = total.astype(BF)
-                    f_copy(n).start()
+                    fs[h, n] = total.astype(BF)
+                    f_copy(h, n).start()
                 return 0
             lax.fori_loop(0, n_out, step, 0)
 
+        side = z // near
         own_sends(0)
-        hops(0)
+        for d in range(1, near):
+            hop(0, d)
+        siblings(0, side)
+        gate_up(side, arrived(side), 0)
+        hop(0, near)
+        gate_up(side, arrived(side), 1)
+        for d in range(near + 1, n_z):
+            hop(0, d)
         own_sends(1)
-        siblings(0)
-        gate_up(0)
-        hops(1)
-        siblings(1)
-        gate_up(1)
-        hidden(0)
+        siblings(0, 1 - side)
+        gate_up(1 - side, arrived(1 - side), 0)
+        for d in range(1, near):
+            hop(1, d)
+        gate_up(1 - side, arrived(1 - side), 1)
+        hop(1, near)
+        hidden(side)
+        for d in range(near + 1, n_z):
+            hop(1, d)
+        siblings(1, 0)
+        siblings(1, 1)
         o_copy.wait_recv()
-        sort(0)
-        down(0)
-        hidden(1)
-        sort(1)
-        down(1)
+        sort_tokens()
+        hidden(1 - side)
+        gate_up(2, lambda q: xt[0, q], 0)
+        gate_up(2, lambda q: xt[0, q], 1)
+        hidden_arrival(0)
+        hidden_arrival(1)
+        sort_hidden()
+        down((0, 1))
+        gate_up(3, lambda q: xt[1, q], 0)
+        gate_up(3, lambda q: xt[1, q], 1, True)
+        hidden(2)
+        hidden(3)
         finish(0)
         finish(1)
-
-        def last(n, _):
-            f_copy(n).wait_recv()
-            out[:, pl.ds(pl.multiple_of(ox * out_w + n * span, span), span)] = fr[n]
-            return 0
-        lax.fori_loop(0, n_out, last, 0)
+        hidden_arrival(2)
+        in_order(2)
+        down((2,))
+        hidden_arrival(3)
+        in_order(3)
+        down((3,), True)
+        finish(2)
+        finish(3)
+
+        for h in range(2):
+            def last(n, _):
+                f_copy(h, n).wait_recv()
+                out[h * share:(h + 1) * share,
+                    pl.ds(pl.multiple_of(ox * out_w + n * span, span), span)] = fr[h, n]
+                return 0
+            lax.fori_loop(0, n_out, last, 0)
 
         x_copy.wait_send()
         o_copy.wait_send()
@@ -340,56 +393,61 @@
             for d in range(n_z):
                 ag_each(b, d, sent)
 
+        def sent_unit(u, _):
             def sent_x(j, _):
-                p_copy(b, j).wait_send()
-                h_copy(b, j, x).wait_send()
+                p_copy(u, j).wait_send()
+                h_copy(u, j, x).wait_send()
                 return 0
             lax.fori_loop(0, n_half, sent_x, 0)
 
             def sent_z(n, _):
-                q_copy(b, n).wait_send()
+                q_copy(u, n).wait_send()
                 for o in range(1, n_z):
-                    z_copy(b, n, o).wait_send()
+                    z_copy(u, n, o).wait_send()
                 return 0
             lax.fori_loop(0, n_out, sent_z, 0)
+            return 0
+        lax.fori_loop(0, 4, sent_unit, 0)
 
         def sent_f(n, _):
-            f_copy(n).wait_send()
+            f_copy(0, n).wait_send()
+            f_copy(1, n).wait_send()
             return 0
         lax.fori_loop(0, n_out, sent_f, 0)
 
     z, c = lax.axis_index("tensor"), lax.axis_index("pair")
     kinds = lax.dynamic_slice_in_dim(modality, z * held, held, 0)
     kinds = jnp.broadcast_to(kinds[:, None], (held, 128))
-    order = time_order.reshape(n_z, 2, share).transpose(1, 0, 2)
-    order = jnp.where(c == 0, order, order[::-1]).reshape(1, rows)
+    order = time_order.reshape(n_z, 2, 2, share).transpose(2, 1, 0, 3)
+    order = jnp.where(c == 0, order, order[:, ::-1]).reshape(1, rows)
     order = jnp.broadcast_to(order, (8, rows))
     vmem, anywhere = pl.BlockSpec(memory_space=pltpu.VMEM), pl.BlockSpec(memory_space=pl.ANY)
     dma = pltpu.SemaphoreType.DMA
     scratch = [
         pltpu.VMEM((held, quarter), BF),
         pltpu.VMEM((2, 2, rows, quarter), BF),
+        pltpu.VMEM((2, 2, half_rows, quarter), BF),
         pltpu.VMEM((8, rows), jnp.int32),
         pltpu.VMEM((2, 2, depth, wide), BF),
         pltpu.VMEM((2, units, span), BF),
-        pltpu.VMEM((2, n_half, 2, rows, wide), BF),
-        pltpu.VMEM((2, n_half, 2, rows, wide), BF),
-        pltpu.VMEM((2, n_half, 2, rows, wide), F32),
-        pltpu.VMEM((2, 2 * n_half, rows, wide), BF),
+        pltpu.VMEM((4, n_half, 2, half_rows, wide), BF),
+        pltpu.VMEM((4, n_half, 2, half_rows, wide), BF),
+        pltpu.VMEM((4, n_half, 2, half_rows, wide), F32),
+        pltpu.VMEM((4, 2 * n_half, half_rows, wide), BF),
         pltpu.VMEM((rows, units), BF),
-        pltpu.VMEM((2, n_out, half_rows, span), BF),
-        pltpu.VMEM((2, n_out, half_rows, span), BF),
-        pltpu.VMEM((2, half_rows, span), F32),
-        pltpu.VMEM((2, n_out, half_rows, span), BF),
-        pltpu.VMEM((2, n_out, n_z, share, span), BF),
-        pltpu.VMEM((2, n_out, share, span), F32),
-        pltpu.VMEM((n_out, share, span), BF),
-        pltpu.VMEM((n_out, share, span), BF),
+        pltpu.VMEM((4, n_out, kept, span), BF),
+        pltpu.VMEM((4, n_out, kept, span), BF),
+        pltpu.VMEM((2, 2, kept, span), F32),
+        pltpu.VMEM((4, n_out, kept, span), BF),
+        pltpu.VMEM((4, n_out, n_z, share, span), BF),
+        pltpu.VMEM((4, n_out, share, span), F32),
+        pltpu.VMEM((2, n_out, share, span), BF),
+        pltpu.VMEM((2, n_out, share, span), BF),
         dma((2, 2)), dma((2,)), dma, dma, dma, dma,
         dma((2, n_z, 3)), dma((2, n_z)), dma((2, n_z)),
-        dma((2, n_half)), dma((2, n_half)), dma((2, n_half)), dma((2, n_half)),
-        dma((2, n_out)), dma((2, n_out)), dma((2, n_out, n_z)), dma((2, n_out, n_z)),
-        dma((n_out,)), dma((n_out,)),
+        dma((4, n_half)), dma((4, n_half)), dma((4, n_half)), dma((4, n_half)),
+        dma((4, n_out)), dma((4, n_out)), dma((4, n_out, n_z)), dma((4, n_out, n_z)),
+        dma((2, n_out)), dma((2, n_out)),
     ]
     return pl.pallas_call(
         kernel,
@@ -417,7 +475,7 @@
 
     def per_device(*arrays):
         share = arrays[1].shape[0] // (mesh.shape["tensor"] * mesh.shape["pair"])
-        if mesh.shape["dp"] == 2 and mesh.shape["pair"] == 2 and share % 16 == 0:
+        if mesh.shape["dp"] == 2 and mesh.shape["pair"] == 2 and share % 32 == 0:
             return fused(mesh, *arrays)
         return plain(mesh, *arrays)
 

time: 147 us -> 139 us (0.946)
  Pallas kernels: 142 us -> 133 us
    pallas_call x1, Pallas kernels: 142 us -> 133 us  [fused(): pl.pallas_call(kernel, out_shape=jax.ShapeDtypeStruct((rows // (n_z * 2),...]
where the time goes in v3:
time: 139 us; the launch traced here: 138 us
  Pallas kernels  133 us (96%)
  local copies, waits for them, and re-layouts  4.76 us (3%)
    pallas_call x1, Pallas kernels, fused(): pl.pallas_call(kernel, out_shape=jax.ShapeDtypeStruct((rows // (n_z * 2),...  133 us

profile of v3, /device:TPU:0, one launch (start us, length us, event | category | flops | bytes accessed | tf_op | source)
XLA Modules:
  0.0 138.1 jit_solution(9146111228992642663)
XLA Ops:
  0.0 0.8 dynamic_slice.3
  0.8 0.8 reshape.6
  1.5 0.1 broadcast_in_dim.14
  1.6 0.6 broadcast_in_dim.15.order
  2.2 0.7 broadcast_in_dim.6.kinds
  2.9 133.3 %shard_map.73 = bf16[32,8192]{1,0:T(8,128)(2,1)} custom-call(bf16[64,8192]{1,0:T(8,128)(2,1)} %tok.1, s32[64,128]{1,0:T(8,128)} %broadcast_in_dim.6.kinds, s32[8,256]{1,0:T(8,128)} %broadcast_in_dim.15.order, f32[2,8192]{1,0:T(2,128)} %gain.1, bf16[4096,2048]{1,0:T(8,128)(2,1)} %gw.1, bf16[4096,2048]{1,0:T(8,128)(2,1)} %uw.1, bf16[2048,4096]{1,0:T(8,128)(2,1)} %dw.1), custom_call_target="tpu_custom_call" | custom-call | flops 25769803776 | bytes 100663296 | tf_op jit(solution)/shard_map/pallas_call | solution.py:452
  136.2 1.9 %copy.10 = bf16[32,8192]{1,0:T(8,128)(2,1)} copy(bf16[32,8192]{1,0:T(8,128)(2,1)} %shard_map.73) | data formatting | bytes 1048576
  (2 shorter events, 0.0 us)

commit v4 on v3

--- a/solution.py
+++ b/solution.py
@@ -106,12 +106,17 @@
             for copy in gu_copies(j, slot):
                 copy.start()
 
-        def down_copy(n, slot):
+        def down_copy(n):
             col = pl.multiple_of(n * span, span)
-            return pltpu.make_async_copy(dw.at[:, pl.ds(col, span)], wdb.at[slot], dsem.at[slot])
+            return pltpu.make_async_copy(dw.at[:, pl.ds(col, span)], wdb.at[n], dsem.at[n])
+
+        def down_load():
+            def step(n, _):
+                down_copy(n).start()
+                return 0
+            lax.fori_loop(0, n_out, step, 0)
 
         gu_start(0, 0)
-        down_copy(0, 0).start()
 
         barrier = pltpu.get_barrier_semaphore()
         pl.semaphore_signal(barrier, inc=1, device_id={"dp": ox}, device_id_type=MESH)
@@ -196,7 +201,7 @@
         def p_copy(u, j):
             return remote(ps.at[u, j], pr.at[u, j], p_s.at[u, j], p_r.at[u, j], dp=ox)
 
-        def gate_up(u, rows_of, part, final=False):
+        def gate_up(units_of, rows_of, part, final=False):
             def step(j, _):
                 slot = lax.rem(j, 2)
                 if final:
@@ -208,12 +213,14 @@
                 for m in range(2):
                     got = (jnp.dot(rows_of(0), wgb[slot, m, :quarter, :], preferred_element_type=F32)
                            + jnp.dot(rows_of(1), wgb[slot, m, quarter:, :], preferred_element_type=F32))
-                    if part == 0:
-                        ps[u, j, m] = got.astype(BF)
-                    else:
-                        own[u, j - n_half, m] = got
+                    for i, u in enumerate(units_of):
+                        if part == 0:
+                            ps[u, j, m] = got[i * half_rows:(i + 1) * half_rows].astype(BF)
+                        else:
+                            own[u, j - n_half, m] = got[i * half_rows:(i + 1) * half_rows]
                 if part == 0:
-                    p_copy(u, j).start()
+                    for u in units_of:
+                        p_copy(u, j).start()
                 return 0
             lax.fori_loop(part * n_half, (part + 1) * n_half, step, 0)
 
@@ -258,8 +265,7 @@
             for q in range(2):
                 for k in range(0, quarter, span):
                     moved = jnp.dot(chosen, xg[1, q, :, k:k + span], preferred_element_type=F32).astype(BF)
-                    xt[0, q, :, k:k + span] = moved[:half_rows]
-                    xt[1, q, :, k:k + span] = moved[half_rows:]
+                    xt[q, :, k:k + span] = moved
 
         def in_order(u):
             for k in range(2 * n_half):
@@ -289,17 +295,14 @@
                 keep[slot, i] = total
                 acc[u, n] = keep[slot, i, pl.ds(pl.multiple_of(z * share, share), share), :]
 
-        def down(units_of, final=False):
+        def down(units_of, loads=False):
             many = len(units_of)
 
             def step(n, _):
                 slot = lax.rem(n, 2)
-                if final:
-                    pl.when(n + 1 < n_out)(lambda: down_copy(n + 1, 1 - slot).start())
-                else:
-                    down_copy(lax.rem(n + 1, n_out), 1 - slot).start()
-                down_copy(n, slot).wait()
-                part = jnp.dot(sh[:many * half_rows, :], wdb[slot], preferred_element_type=F32)
+                if loads:
+                    down_copy(n).wait()
+                part = jnp.dot(sh[:many * half_rows, :], wdb[n], preferred_element_type=F32)
                 for i, u in enumerate(units_of):
                     qs[u, n] = part[i * half_rows + kept:(i + 1) * half_rows].astype(BF)
                     q_copy(u, n).start()
@@ -338,17 +341,18 @@
         for d in range(1, near):
             hop(0, d)
         siblings(0, side)
-        gate_up(side, arrived(side), 0)
+        gate_up((side,), arrived(side), 0)
         hop(0, near)
-        gate_up(side, arrived(side), 1)
+        gate_up((side,), arrived(side), 1)
         for d in range(near + 1, n_z):
             hop(0, d)
         own_sends(1)
         siblings(0, 1 - side)
-        gate_up(1 - side, arrived(1 - side), 0)
+        gate_up((1 - side,), arrived(1 - side), 0)
         for d in range(1, near):
             hop(1, d)
-        gate_up(1 - side, arrived(1 - side), 1)
+        gate_up((1 - side,), arrived(1 - side), 1)
+        down_load()
         hop(1, near)
         hidden(side)
         for d in range(near + 1, n_z):
@@ -358,26 +362,22 @@
         o_copy.wait_recv()
         sort_tokens()
         hidden(1 - side)
-        gate_up(2, lambda q: xt[0, q], 0)
-        gate_up(2, lambda q: xt[0, q], 1)
+        gate_up((2, 3), lambda q: xt[q], 0)
         hidden_arrival(0)
         hidden_arrival(1)
         sort_hidden()
-        down((0, 1))
-        gate_up(3, lambda q: xt[1, q], 0)
-        gate_up(3, lambda q: xt[1, q], 1, True)
+        down((0, 1), True)
+        gate_up((2, 3), lambda q: xt[q], 1, True)
         hidden(2)
         hidden(3)
-        finish(0)
-        finish(1)
         hidden_arrival(2)
         in_order(2)
         down((2,))
         hidden_arrival(3)
         in_order(3)
-        down((3,), True)
-        finish(2)
-        finish(3)
+        down((3,))
+        for u in range(4):
+            finish(u)
 
         for h in range(2):
             def last(n, _):
@@ -426,10 +426,10 @@
     scratch = [
         pltpu.VMEM((held, quarter), BF),
         pltpu.VMEM((2, 2, rows, quarter), BF),
-        pltpu.VMEM((2, 2, half_rows, quarter), BF),
+        pltpu.VMEM((2, rows, quarter), BF),
         pltpu.VMEM((8, rows), jnp.int32),
         pltpu.VMEM((2, 2, depth, wide), BF),
-        pltpu.VMEM((2, units, span), BF),
+        pltpu.VMEM((n_out, units, span), BF),
         pltpu.VMEM((4, n_half, 2, half_rows, wide), BF),
         pltpu.VMEM((4, n_half, 2, half_rows, wide), BF),
         pltpu.VMEM((4, n_half, 2, half_rows, wide), F32),
@@ -443,7 +443,7 @@
         pltpu.VMEM((4, n_out, share, span), F32),
         pltpu.VMEM((2, n_out, share, span), BF),
         pltpu.VMEM((2, n_out, share, span), BF),
-        dma((2, 2)), dma((2,)), dma, dma, dma, dma,
+        dma((2, 2)), dma((n_out,)), dma, dma, dma, dma,
         dma((2, n_z, 3)), dma((2, n_z)), dma((2, n_z)),
         dma((4, n_half)), dma((4, n_half)), dma((4, n_half)), dma((4, n_half)),
         dma((4, n_out)), dma((4, n_out)), dma((4, n_out, n_z)), dma((4, n_out, n_z)),
@@ -456,7 +456,7 @@
         out_specs=vmem,
         scratch_shapes=scratch,
         compiler_params=pltpu.CompilerParams(
-            collective_id=0, has_side_effects=True, vmem_limit_bytes=58 * 2**20),
+            collective_id=0, has_side_effects=True, vmem_limit_bytes=60 * 2**20),
         cost_estimate=pl.CostEstimate(
             flops=12 * rows * depth * units, bytes_accessed=12 * depth * units, transcendentals=0),
     )(tokens, kinds, order, norm_gain, gate_weight, up_weight, down_weight)

time: 139 us -> 128 us (0.921)
  Pallas kernels: 133 us -> 123 us
    pallas_call x1, Pallas kernels: 133 us -> 123 us  [fused(): pl.pallas_call(kernel, out_shape=jax.ShapeDtypeStruct((rows // (n_z * 2),...]
where the time goes in v4:
time: 128 us
  Pallas kernels  123 us (96%)
  local copies, waits for them, and re-layouts  4.76 us (4%)
    pallas_call x1, Pallas kernels, fused(): pl.pallas_call(kernel, out_shape=jax.ShapeDtypeStruct((rows // (n_z * 2),...  123 us

profile of v4, /device:TPU:0, one launch (start us, length us, event | category | flops | bytes accessed | tf_op | source)
XLA Modules:
  0.0 128.2 jit_solution(18068797224000824784)
XLA Ops:
  0.0 0.8 dynamic_slice.3
  0.8 0.8 reshape.6
  1.5 0.1 broadcast_in_dim.14
  1.6 0.6 broadcast_in_dim.15.order
  2.2 0.7 broadcast_in_dim.6.kinds
  2.9 123.4 %shard_map.73 = bf16[32,8192]{1,0:T(8,128)(2,1)} custom-call(bf16[64,8192]{1,0:T(8,128)(2,1)} %tok.1, s32[64,128]{1,0:T(8,128)} %broadcast_in_dim.6.kinds, s32[8,256]{1,0:T(8,128)} %broadcast_in_dim.15.order, f32[2,8192]{1,0:T(2,128)} %gain.1, bf16[4096,2048]{1,0:T(8,128)(2,1)} %gw.1, bf16[4096,2048]{1,0:T(8,128)(2,1)} %uw.1, bf16[2048,4096]{1,0:T(8,128)(2,1)} %dw.1), custom_call_target="tpu_custom_call" | custom-call | flops 25769803776 | bytes 100663296 | tf_op jit(solution)/shard_map/pallas_call | solution.py:452
  126.3 1.9 %copy.10 = bf16[32,8192]{1,0:T(8,128)(2,1)} copy(bf16[32,8192]{1,0:T(8,128)(2,1)} %shard_map.73) | data formatting | bytes 1048576
  (2 shorter events, 0.0 us)

commit v5 on v4

--- a/solution.py
+++ b/solution.py
@@ -87,9 +87,9 @@
     share = kept // n_z
 
     def kernel(tok, kinds, order, gain, gw, uw, dw, out,
-               xs, xg, xt, order2, wgb, wdb, ps, pr, own, hid, sh, qs, qr, keep, zs, zr, acc, fs, fr,
+               xs, xg, xt, order2, wgb, wdb, ps, pr, own, hid, sh, qs, qr, keep, zs, zr, zs2, zr2, acc, fs, fr,
                wsem, dsem, xs_s, xs_r, o_s, o_r, ag_s, ag_rz, ag_rp, p_s, p_r, h_s, h_r,
-               q_s, q_r, z_s, z_r, f_s, f_r):
+               q_s, q_r, n_s, n_r, z_s, z_r, f_s, f_r):
         x, z, c = lax.axis_index("dp"), lax.axis_index("tensor"), lax.axis_index("pair")
         ox, oc = 1 - x, 1 - c
 
@@ -274,15 +274,15 @@
         def q_copy(u, n):
             return remote(qs.at[u, n], qr.at[u, n], q_s.at[u, n], q_r.at[u, n], pair=oc)
 
-        def z_copy(u, n, o):
-            to = lax.rem(z + o, n_z)
-            return remote(zs.at[u, n, pl.ds(pl.multiple_of(to * share, share), share)], zr.at[u, n, z],
-                          z_s.at[u, n, o], z_r.at[u, n, z], tensor=to)
-
-        def z_arrival(u, n, o):
-            src = lax.rem(z + o, n_z)
-            return remote(zs.at[u, n, pl.ds(0, share)], zr.at[u, n, src],
-                          z_s.at[u, n, o], z_r.at[u, n, src], tensor=src)
+        low, high = lax.rem(z, 2), z // 2
+
+        def near_copy(u, n):
+            mine = zs.at[u, n, pl.ds(pl.multiple_of((1 - low) * 2 * share, 2 * share), 2 * share)]
+            return remote(mine, zr.at[u, n], n_s.at[u, n], n_r.at[u, n], tensor=z + 1 - 2 * low)
+
+        def far_copy(u, n):
+            mine = zs2.at[u, n, pl.ds(pl.multiple_of((1 - high) * share, share), share)]
+            return remote(mine, zr2.at[u, n], z_s.at[u, n], z_r.at[u, n], tensor=lax.rem(z + 2, n_z))
 
         def reduce(units_of, n):
             slot = lax.rem(n, 2)
@@ -290,12 +290,24 @@
                 q_copy(u, n).wait_recv()
                 total = keep[slot, i] + qr[u, n].astype(F32)
                 zs[u, n] = total.astype(BF)
-                for o in range(1, n_z):
-                    z_copy(u, n, o).start()
+                near_copy(u, n).start()
                 keep[slot, i] = total
-                acc[u, n] = keep[slot, i, pl.ds(pl.multiple_of(z * share, share), share), :]
-
-        def down(units_of, loads=False):
+                acc[u, n] = keep[slot, i, pl.ds(pl.multiple_of(low * 2 * share, 2 * share), 2 * share), :]
+
+        def relay(u, n):
+            near_copy(u, n).wait_recv()
+            total = acc[u, n] + zr[u, n].astype(F32)
+            acc[u, n] = total
+            zs2[u, n] = total.astype(BF)
+            far_copy(u, n).start()
+
+        def relays(u):
+            def step(n, _):
+                relay(u, n)
+                return 0
+            lax.fori_loop(0, n_out, step, 0)
+
+        def down(units_of, loads=False, passing=None):
             many = len(units_of)
 
             def step(n, _):
@@ -308,6 +320,8 @@
                     q_copy(u, n).start()
                     keep[slot, i] = part[i * half_rows:i * half_rows + kept]
                 pl.when(n >= 1)(lambda: reduce(units_of, n - 1))
+                if passing is not None:
+                    relay(passing, n)
                 return 0
             lax.fori_loop(0, n_out, step, 0)
             reduce(units_of, n_out - 1)
@@ -319,10 +333,8 @@
             b, h = u // 2, u % 2
 
             def step(n, _):
-                total = acc[u, n]
-                for o in range(1, n_z):
-                    z_arrival(u, n, o).wait_recv()
-                    total = total + zr[u, n, lax.rem(z + o, n_z)].astype(F32)
+                far_copy(u, n).wait_recv()
+                total = acc[u, n, pl.ds(pl.multiple_of(high * share, share), share), :] + zr2[u, n].astype(F32)
 
                 @pl.when(x == b)
                 def _():
@@ -370,14 +382,19 @@
         gate_up((2, 3), lambda q: xt[q], 1, True)
         hidden(2)
         hidden(3)
+        relays(0)
+        relays(1)
         hidden_arrival(2)
         in_order(2)
         down((2,))
         hidden_arrival(3)
         in_order(3)
-        down((3,))
-        for u in range(4):
-            finish(u)
+        down((3,), passing=2)
+        finish(0)
+        finish(1)
+        relays(3)
+        finish(2)
+        finish(3)
 
         for h in range(2):
             def last(n, _):
@@ -402,8 +419,8 @@
 
             def sent_z(n, _):
                 q_copy(u, n).wait_send()
-                for o in range(1, n_z):
-                    z_copy(u, n, o).wait_send()
+                near_copy(u, n).wait_send()
+                far_copy(u, n).wait_send()
                 return 0
             lax.fori_loop(0, n_out, sent_z, 0)
             return 0
@@ -418,7 +435,7 @@
     z, c = lax.axis_index("tensor"), lax.axis_index("pair")
     kinds = lax.dynamic_slice_in_dim(modality, z * held, held, 0)
     kinds = jnp.broadcast_to(kinds[:, None], (held, 128))
-    order = time_order.reshape(n_z, 2, 2, share).transpose(2, 1, 0, 3)
+    order = time_order.reshape(2, 2, 2, 2, share).transpose(3, 2, 1, 0, 4)
     order = jnp.where(c == 0, order, order[:, ::-1]).reshape(1, rows)
     order = jnp.broadcast_to(order, (8, rows))
     vmem, anywhere = pl.BlockSpec(memory_space=pltpu.VMEM), pl.BlockSpec(memory_space=pl.ANY)
@@ -439,14 +456,16 @@
         pltpu.VMEM((4, n_out, kept, span), BF),
         pltpu.VMEM((2, 2, kept, span), F32),
         pltpu.VMEM((4, n_out, kept, span), BF),
-        pltpu.VMEM((4, n_out, n_z, share, span), BF),
-        pltpu.VMEM((4, n_out, share, span), F32),
+        pltpu.VMEM((4, n_out, 2 * share, span), BF),
+        pltpu.VMEM((4, n_out, 2 * share, span), BF),
+        pltpu.VMEM((4, n_out, share, span), BF),
+        pltpu.VMEM((4, n_out, 2 * share, span), F32),
         pltpu.VMEM((2, n_out, share, span), BF),
         pltpu.VMEM((2, n_out, share, span), BF),
         dma((2, 2)), dma((n_out,)), dma, dma, dma, dma,
         dma((2, n_z, 3)), dma((2, n_z)), dma((2, n_z)),
         dma((4, n_half)), dma((4, n_half)), dma((4, n_half)), dma((4, n_half)),
-        dma((4, n_out)), dma((4, n_out)), dma((4, n_out, n_z)), dma((4, n_out, n_z)),
+        dma((4, n_out)), dma((4, n_out)), dma((4, n_out)), dma((4, n_out)), dma((4, n_out)), dma((4, n_out)),
         dma((2, n_out)), dma((2, n_out)),
     ]
     return pl.pallas_call(
@@ -475,7 +494,7 @@
 
     def per_device(*arrays):
         share = arrays[1].shape[0] // (mesh.shape["tensor"] * mesh.shape["pair"])
-        if mesh.shape["dp"] == 2 and mesh.shape["pair"] == 2 and share % 32 == 0:
+        if mesh.shape["dp"] == 2 and mesh.shape["pair"] == 2 and mesh.shape["tensor"] == 4 and share % 32 == 0:
             return fused(mesh, *arrays)
         return plain(mesh, *arrays)
 

time: 128 us -> 126 us (0.984)
  Pallas kernels: 123 us -> 121 us
    pallas_call x1, Pallas kernels: 123 us -> 121 us  [fused(): pl.pallas_call(kernel, out_shape=jax.ShapeDtypeStruct((rows // (n_z * 2),...]
where the time goes in v5:
time: 126 us
  Pallas kernels  121 us (96%)
  local copies, waits for them, and re-layouts  4.76 us (4%)
    pallas_call x1, Pallas kernels, fused(): pl.pallas_call(kernel, out_shape=jax.ShapeDtypeStruct((rows // (n_z * 2),...  121 us

profile of v5, /device:TPU:0, one launch (start us, length us, event | category | flops | bytes accessed | tf_op | source)
XLA Modules:
  0.0 126.2 jit_solution(604209645484878432)
XLA Ops:
  0.0 0.8 dynamic_slice.3
  0.8 0.8 reshape.6
  1.5 0.1 broadcast_in_dim.14
  1.6 0.6 broadcast_in_dim.15.order
  2.2 0.7 broadcast_in_dim.6.kinds
  2.9 121.4 %shard_map.73 = bf16[32,8192]{1,0:T(8,128)(2,1)} custom-call(bf16[64,8192]{1,0:T(8,128)(2,1)} %tok.1, s32[64,128]{1,0:T(8,128)} %broadcast_in_dim.6.kinds, s32[8,256]{1,0:T(8,128)} %broadcast_in_dim.15.order, f32[2,8192]{1,0:T(2,128)} %gain.1, bf16[4096,2048]{1,0:T(8,128)(2,1)} %gw.1, bf16[4096,2048]{1,0:T(8,128)(2,1)} %uw.1, bf16[2048,4096]{1,0:T(8,128)(2,1)} %dw.1), custom_call_target="tpu_custom_call" | custom-call | flops 25769803776 | bytes 100663296 | tf_op jit(solution)/shard_map/pallas_call | solution.py:471
  124.3 1.9 %copy.10 = bf16[32,8192]{1,0:T(8,128)(2,1)} copy(bf16[32,8192]{1,0:T(8,128)(2,1)} %shard_map.73) | data formatting | bytes 1048576
  (2 shorter events, 0.0 us)

commit v6 on v5

--- a/solution.py
+++ b/solution.py
@@ -219,10 +219,13 @@
                         else:
                             own[u, j - n_half, m] = got[i * half_rows:(i + 1) * half_rows]
                 if part == 0:
-                    for u in units_of:
+                    p_copy(units_of[0], j).start()
+                return 0
+            lax.fori_loop(part * n_half, (part + 1) * n_half, step, 0)
+            if part == 0:
+                for u in units_of[1:]:
+                    for j in range(n_half):
                         p_copy(u, j).start()
-                return 0
-            lax.fori_loop(part * n_half, (part + 1) * n_half, step, 0)
 
         def arrived(half):
             at = pl.ds(pl.multiple_of(half * half_rows, half_rows), half_rows)
@@ -363,10 +366,10 @@
         gate_up((1 - side,), arrived(1 - side), 0)
         for d in range(1, near):
             hop(1, d)
+        hidden(side)
         gate_up((1 - side,), arrived(1 - side), 1)
         down_load()
         hop(1, near)
-        hidden(side)
         for d in range(near + 1, n_z):
             hop(1, d)
         siblings(1, 0)

time: 126 us -> 127 us (level)
  no operation moved by 1% of the time
where the time goes in v6:
time: 127 us
  Pallas kernels  122 us (96%)
  local copies, waits for them, and re-layouts  4.76 us (4%)
    pallas_call x1, Pallas kernels, fused(): pl.pallas_call(kernel, out_shape=jax.ShapeDtypeStruct((rows // (n_z * 2),...  122 us

profile of v6, /device:TPU:0, one launch (start us, length us, event | category | flops | bytes accessed | tf_op | source)
XLA Modules:
  0.0 126.6 jit_solution(13827291364930567066)
XLA Ops:
  0.0 0.8 dynamic_slice.3
  0.8 0.8 reshape.6
  1.5 0.1 broadcast_in_dim.14
  1.6 0.6 broadcast_in_dim.15.order
  2.2 0.7 broadcast_in_dim.6.kinds
  2.9 121.8 %shard_map.73 = bf16[32,8192]{1,0:T(8,128)(2,1)} custom-call(bf16[64,8192]{1,0:T(8,128)(2,1)} %tok.1, s32[64,128]{1,0:T(8,128)} %broadcast_in_dim.6.kinds, s32[8,256]{1,0:T(8,128)} %broadcast_in_dim.15.order, f32[2,8192]{1,0:T(2,128)} %gain.1, bf16[4096,2048]{1,0:T(8,128)(2,1)} %gw.1, bf16[4096,2048]{1,0:T(8,128)(2,1)} %uw.1, bf16[2048,4096]{1,0:T(8,128)(2,1)} %dw.1), custom_call_target="tpu_custom_call" | custom-call | flops 25769803776 | bytes 100663296 | tf_op jit(solution)/shard_map/pallas_call | solution.py:474
  124.7 1.9 %copy.10 = bf16[32,8192]{1,0:T(8,128)(2,1)} copy(bf16[32,8192]{1,0:T(8,128)(2,1)} %shard_map.73) | data formatting | bytes 1048576
  (2 shorter events, 0.0 us)
